TPU v7x, 32 devices: a whole 2x2x4 slice. The times are simulated.
32 devices in a mesh: gy: 8 (over z, y), gz: 4 (over x, core).
Axes of the slice: x: 2, y: 2, z: 4, core: 2. Of those that a mesh axis runs over, the one named last changes fastest.
Arguments:
- velocity: float32 [3, 2, 512, 1024], P(None, None, 'gy', 'gz'), may hold values from -6 to 6
Outputs:
- deriv_y: float32 [3, 2, 512, 1024], P(None, None, 'gy', 'gz')
- deriv_z: float32 [3, 2, 512, 1024], P(None, None, 'gy', 'gz')
All inputs are finite; a program needn't handle non-finite values.
Results may differ from a plain program's by a relative error of at most 0.00007.
Values sent between devices are 32-bit elements; how exact they have to be, the bound alone decides.
A program may use at most 64 MiB of HBM per device.

v0:
```python
import math

import jax
import jax.numpy as jnp
from jax import lax
from jax.sharding import PartitionSpec as P

coef_near = 7.0 / 9.0
coef_far = 1.0 / 36.0
alpha_side = 1.0 / 3.0
ratio_root = 1.5 - math.sqrt(5.0) / 2.0
margin_cells = 24
best = lax.Precision.HIGHEST


def padded_2(block, sides, width):
    for axis, dim in sides:
        count = lax.axis_size(axis)
        forward = [(i, i + 1) for i in range(count - 1)]
        forward.append((count - 1, 0))
        backward = [(target, source) for source, target in forward]
        low = lax.ppermute(
            lax.slice_in_dim(block, block.shape[dim] - width, None, axis=dim), axis, forward
        )
        high = lax.ppermute(lax.slice_in_dim(block, 0, width, axis=dim), axis, backward)
        block = jnp.concatenate([low, block, high], axis=dim)
    return block


def shifted(shard, axis, by):
    count = lax.axis_size(axis)
    return lax.ppermute(shard, axis, [(i, (i + by) % count) for i in range(count)])


def alternating(power):
    signs = jnp.where(power % 2 == 0, 1.0, -1.0).astype(jnp.float32)
    return signs * jnp.power(jnp.float32(ratio_root), power.astype(jnp.float32))


def explicit(padded, axis):
    length = padded.shape[axis] - 4

    def part(start):
        return lax.slice_in_dim(padded, start, start + length, axis=axis)

    return coef_near * (part(3) - part(1)) + coef_far * (part(4) - part(0))


def green_window(count):
    rows = jnp.arange(count, dtype=jnp.int32)[:, None]
    cols = jnp.arange(count + 2 * margin_cells, dtype=jnp.int32)[None, :]
    spread = jnp.abs(rows + margin_cells - cols)
    scale = ratio_root / alpha_side / (1.0 - ratio_root * ratio_root)
    return scale * alternating(spread)


def y_chain(velocity):
    count = velocity.shape[2]
    padded = padded_2(velocity, (("gy", 2),), 2)
    rhs_rows = explicit(padded, 2)
    rows = jnp.arange(count, dtype=jnp.int32)[:, None]
    cols = jnp.arange(count, dtype=jnp.int32)[None, :]
    distance = jnp.abs(rows - cols)
    lower = jnp.where(rows >= cols, ratio_root / alpha_side * alternating(distance), 0.0)
    upper = jnp.where(cols >= rows, alternating(distance), 0.0)
    places = jnp.arange(count, dtype=jnp.int32)
    head_decay = alternating(places + 1)
    tail_decay = alternating(count - places)
    forward = jnp.einsum("ij,cxjz->cxiz", lower, rhs_rows, precision=best)
    carry_in = shifted(forward[:, :, -1, :], "gy", 1)
    forward = forward + head_decay[None, None, :, None] * carry_in[:, :, None, :]
    backward = jnp.einsum("ij,cxjz->cxiz", upper, forward, precision=best)
    carry_back = shifted(backward[:, :, 0, :], "gy", -1)
    return backward + tail_decay[None, None, :, None] * carry_back[:, :, None, :]


def z_margin(velocity):
    padded = padded_2(velocity, (("gz", 3),), margin_cells + 2)
    rhs_cols = explicit(padded, 3)
    window = green_window(velocity.shape[3])
    return jnp.einsum("ij,cxyj->cxyi", window, rhs_cols, precision=best)


def per_device(velocity):
    deriv_y = y_chain(velocity)
    deriv_z = z_margin(velocity)
    return (deriv_y, deriv_z)


def solution(mesh):
    in_specs = (P(None, None, "gy", "gz"),)
    out_specs = (P(None, None, "gy", "gz"), P(None, None, "gy", "gz"))
    return jax.shard_map(
        per_device, mesh=mesh, in_specs=in_specs, out_specs=out_specs, check_vma=False
    )
```

profile of v0, /device:TPU:0, one launch (start us, length us, event | category | flops | bytes accessed | tf_op | source)
XLA Modules:
  0.0 28.5 jit_solution(7270939064529452850)
XLA Ops:
  0.6 0.8 %fusion.103 = (f32[3,2,2,256]{3,2,1,0:T(2,128)S(1)}, f32[3,2,2,256]{3,2,1,0:T(2,128)S(1)}) fusion(f32[3,2,64,256]{3,2,1,0:T(8,128)} %param.1), kind=kLoop, calls=%fused_computation.126 | loop fusion | bytes 49152 | tf_op jit(solution)/shard_map/slice | solution.py:25
  1.5 6.1 %collective-permute-start = (f32[3,2,2,256]{3,2,1,0:T(2,128)S(1)}, f32[3,2,2,256]{3,2,1,0:T(2,128)S(1)}, u32[]{:S(2)}, u32[]{:S(2)}) collective-permute-start(f32[3,2,2,256]{3,2,1,0:T(2,128)S(1)} %get-tuple-element.4), channel_id=1, source_target_pairs={{4,0},{8,4},{12,8},{16,12},{20,16},{24,20},{28,24},{0,28},{5,1},{9... | collective-permute-start | bytes 36872 | tf_op jit(solution)/shard_map/ppermute | solution.py:25
  7.5 0.0 copy-start
  7.5 0.0 collective-permute-start.1
  7.5 1.2 %fusion.102 = (f32[3,2,64,26]{3,2,1,0:T(8,128)S(1)}, f32[3,2,64,26]{3,2,1,0:T(8,128)S(1)}) fusion(f32[3,2,64,256]{3,2,1,0:T(8,128)} %param.1), kind=kLoop, calls=%fused_computation.125 | loop fusion | bytes 159744 | tf_op jit(solution)/shard_map/slice | solution.py:23
  8.7 0.1 collective-permute-start.4
  8.8 1.7 %collective-permute-start.5 = (f32[3,2,64,26]{3,2,1,0:T(8,128)S(1)}, f32[3,2,64,26]{3,2,1,0:T(8,128)S(1)}, u32[]{:S(2)}, u32[]{:S(2)}) collective-permute-start(f32[3,2,64,26]{3,2,1,0:T(8,128)S(1)} %get-tuple-element.3), channel_id=1, source_target_pairs={{1,0},{2,1},{3,2},{0,3},{5,4},{6,5},{7,6},{4,7},{9,8},{10,9},{11,1... | collective-permute-start | bytes 119816 | tf_op jit(solution)/shard_map/ppermute | solution.py:25
  10.5 0.0 copy-done
  10.6 0.0 collective-permute-done
  10.6 3.3 %collective-permute-done.1 = f32[3,2,2,256]{3,2,1,0:T(2,128)S(1)} collective-permute-done((f32[3,2,2,256]{3,2,1,0:T(2,128)S(1)}, f32[3,2,2,256]{3,2,1,0:T(2,128)S(1)}, u32[]{:S(2)}, u32[]{:S(2)}) %collective-permute-start.1) | collective-permute-done | bytes 12320 | tf_op jit(solution)/shard_map/ppermute | solution.py:22
  13.9 0.7 %convolution_bitcast_fusion.1 = f32[3,2,64,256]{3,2,1,0:T(8,128)S(1)} fusion(f32[3,2,2,256]{3,2,1,0:T(2,128)S(1)} %collective-permute-done.1, f32[3,2,64,256]{3,2,1,0:T(8,128)S(1)} %copy-done, f32[3,2,66,256]{3,2,1,0:T(8,128)S(1)} %constant_dynamic-update-slice_fusion), kind=kOutput, calls=%fused_computation.1 | convolution fusion | flops 76267520 | bytes 1585152 | tf_op jit(solution)/shard_map/ij,cxjz->cxiz/dot_general | solution.py:69
  14.7 0.1 collective-permute-start.2
  14.7 6.3 %collective-permute-done.2 = f32[3,2,256]{2,1,0:T(2,128)S(1)} collective-permute-done((f32[3,2,256]{2,1,0:T(2,128)S(1)}, f32[3,2,256]{2,1,0:T(2,128)S(1)}, u32[]{:S(2)}, u32[]{:S(2)}) %collective-permute-start.2) | collective-permute-done | bytes 6176 | tf_op jit(solution)/shard_map/ppermute | solution.py:32
  21.0 0.6 %convolution_bitcast_fusion = f32[3,2,64,256]{3,2,1,0:T(8,128)S(1)} fusion(f32[3,2,64,256]{3,2,1,0:T(8,128)S(1)} %convolution_bitcast_fusion.1, f32[3,2,256]{2,1,0:T(2,128)S(1)} %collective-permute-done.2, f32[64]{0:T(128)S(1)} %fusion.71), kind=kOutput, calls=%fused_computation | convolution fusion | flops 75771904 | bytes 792832 | tf_op jit(solution)/shard_map/ij,cxjz->cxiz/dot_general | solution.py:72
  21.6 0.1 collective-permute-start.3
  21.7 3.6 %collective-permute-done.3 = f32[3,2,256]{2,1,0:T(2,128)S(1)} collective-permute-done((f32[3,2,256]{2,1,0:T(2,128)S(1)}, f32[3,2,256]{2,1,0:T(2,128)S(1)}, u32[]{:S(2)}, u32[]{:S(2)}) %collective-permute-start.3) | collective-permute-done | bytes 6176 | tf_op jit(solution)/shard_map/ppermute | solution.py:32
  25.3 0.8 %multiply_add_fusion = f32[3,2,64,256]{3,2,1,0:T(8,128)} fusion(f32[3,2,64,256]{3,2,1,0:T(8,128)S(1)} %convolution_bitcast_fusion, f32[3,2,256]{2,1,0:T(2,128)S(1)} %collective-permute-done.3, f32[64]{0:T(128)S(1)} %fusion.72), kind=kLoop, calls=%fused_computation.26 | loop fusion | flops 196608 | bytes 792832 | tf_op jit(solution)/shard_map/add | solution.py:74
  26.2 0.0 collective-permute-done.4
  26.2 0.0 collective-permute-done.5
  26.2 0.3 pad_maximum_fusion
  26.5 2.1 %fusion.2 = f32[3,2,64,256]{3,2,1,0:T(8,128)} fusion(f32[3,2,64,308]{3,2,1,0:T(8,128)S(1)} %pad_maximum_fusion, s32[256]{0:T(256)S(1)} %iota_add_fusion), kind=kOutput, calls=%fused_computation.5 | convolution fusion | flops 360597504 | bytes 2753536 | tf_op jit(solution)/shard_map/ij,cxyj->cxyi/dot_general | solution.py:81
  (9 shorter events, 0.1 us)
Async XLA Ops:
  1.5 9.1 %collective-permute-start = (f32[3,2,2,256]{3,2,1,0:T(2,128)S(1)}, f32[3,2,2,256]{3,2,1,0:T(2,128)S(1)}, u32[]{:S(2)}, u32[]{:S(2)}) collective-permute-start(f32[3,2,2,256]{3,2,1,0:T(2,128)S(1)} %get-tuple-element.4), channel_id=1, source_target_pairs={{4,0},{8,4},{12,8},{16,12},{20,16},{24,20},{28,24},{0,28},{5,1},{9... | collective-permute-start | bytes 36872 | tf_op jit(solution)/shard_map/ppermute | solution.py:25
  7.5 3.0 %copy-start = (f32[3,2,64,256]{3,2,1,0:T(8,128)S(1)}, f32[3,2,64,256]{3,2,1,0:T(8,128)}, u32[]{:S(2)}) copy-start(f32[3,2,64,256]{3,2,1,0:T(8,128)} %param.1) | copy-start | bytes 1179652
  7.5 6.4 %collective-permute-start.1 = (f32[3,2,2,256]{3,2,1,0:T(2,128)S(1)}, f32[3,2,2,256]{3,2,1,0:T(2,128)S(1)}, u32[]{:S(2)}, u32[]{:S(2)}) collective-permute-start(f32[3,2,2,256]{3,2,1,0:T(2,128)S(1)} %get-tuple-element.5), channel_id=1, source_target_pairs={{0,4},{4,8},{8,12},{12,16},{16,20},{20,24},{24,28},{28,0},{1,5},{5... | collective-permute-start | bytes 36872 | tf_op jit(solution)/shard_map/ppermute | solution.py:22
  8.7 17.5 %collective-permute-start.4 = (f32[3,2,64,26]{3,2,1,0:T(8,128)S(1)}, f32[3,2,64,26]{3,2,1,0:T(8,128)S(1)}, u32[]{:S(2)}, u32[]{:S(2)}) collective-permute-start(f32[3,2,64,26]{3,2,1,0:T(8,128)S(1)} %get-tuple-element.2), channel_id=1, source_target_pairs={{0,1},{1,2},{2,3},{3,0},{4,5},{5,6},{6,7},{7,4},{8,9},{9,10},{10,1... | collective-permute-start | bytes 119816 | tf_op jit(solution)/shard_map/ppermute | solution.py:22
  8.8 17.4 %collective-permute-start.5 = (f32[3,2,64,26]{3,2,1,0:T(8,128)S(1)}, f32[3,2,64,26]{3,2,1,0:T(8,128)S(1)}, u32[]{:S(2)}, u32[]{:S(2)}) collective-permute-start(f32[3,2,64,26]{3,2,1,0:T(8,128)S(1)} %get-tuple-element.3), channel_id=1, source_target_pairs={{1,0},{2,1},{3,2},{0,3},{5,4},{6,5},{7,6},{4,7},{9,8},{10,9},{11,1... | collective-permute-start | bytes 119816 | tf_op jit(solution)/shard_map/ppermute | solution.py:25
  14.7 6.4 %collective-permute-start.2 = (f32[3,2,256]{2,1,0:T(2,128)S(1)}, f32[3,2,256]{2,1,0:T(2,128)S(1)}, u32[]{:S(2)}, u32[]{:S(2)}) collective-permute-start(f32[3,2,256]{2,1,0:T(2,128)S(1)} %bitcast.25), channel_id=1, source_target_pairs={{0,4},{4,8},{8,12},{12,16},{16,20},{20,24},{24,28},{28,0},{1,5},{5... | collective-permute-start | bytes 18440 | tf_op jit(solution)/shard_map/ppermute | solution.py:32
  21.6 3.7 %collective-permute-start.3 = (f32[3,2,256]{2,1,0:T(2,128)S(1)}, f32[3,2,256]{2,1,0:T(2,128)S(1)}, u32[]{:S(2)}, u32[]{:S(2)}) collective-permute-start(f32[3,2,256]{2,1,0:T(2,128)S(1)} %bitcast.26), channel_id=1, source_target_pairs={{0,28},{4,0},{8,4},{12,8},{16,12},{20,16},{24,20},{28,24},{1,29},{... | collective-permute-start | bytes 18440 | tf_op jit(solution)/shard_map/ppermute | solution.py:32
where the time goes:
time: 28.7 us; the launch traced here: 28.5 us
  waiting for transfers between devices  13.2 us (46%)
  starting transfers between devices  7.97 us (28%)
  matrix products  3.35 us (12%)
  local copies, waits for them, and re-layouts  2.08 us (7%)
  other arithmetic  1.15 us (4%)
  between operations  0.76 us (3%)
    ppermute x2, waiting for transfers between devices, shifted(): lax.ppermute(shard, axis, [(i, (i + by) % count) for i in range(count)])  9.9 us
    ppermute x2, starting transfers between devices, padded_2(): lax.ppermute(lax.slice_in_dim(block, 0, width, axis=dim), axis, backward)  7.79 us
    ppermute x2, waiting for transfers between devices, padded_2(): lax.ppermute(lax.slice_in_dim(block, block.shape[dim] - width, None, axis...  3.33 us
    dot_general x1, matrix products, z_margin(): return jnp.einsum('ij,cxyj->cxyi', window, rhs_cols, precision=best)  2.07 us
    slice x1, local copies, waits for them, and re-layouts, padded_2(): lax.slice_in_dim(block, block.shape[dim] - width, None, axis=dim)  1.18 us
    add x1, other arithmetic, y_chain(): backward + tail_decay[None, None, :, None] * carry_back[:, :, None, :]  0.85 us
    slice x1, local copies, waits for them, and re-layouts, padded_2(): lax.slice_in_dim(block, 0, width, axis=dim)  0.84 us
    dot_general x1, matrix products, y_chain(): forward = jnp.einsum('ij,cxjz->cxiz', lower, rhs_rows, precision=best)  0.7 us
  transfers between devices with their start and end apart: 6, of which 3 were waited for; matrix products, arithmetic and copies ran while one was open for 12% of the time, Pallas kernels for 0%

commit v1 on v0

v1 whole, which is shorter than its diff:
```python
import functools
import math

import jax
import jax.numpy as jnp
from jax import lax
from jax.experimental import pallas as pl
from jax.experimental.pallas import tpu as pltpu
from jax.sharding import PartitionSpec as P

MESH = pl.DeviceIdType.MESH
ratio = 1.5 - math.sqrt(5.0) / 2.0
near = 7.0 / 9.0
far = 1.0 / 36.0
green = 1.0 / (1.0 - 2.0 / 3.0 * ratio)
tail = green * (near * (1.0 / ratio - ratio) + far * (ratio**2 - 1.0 / ratio**2))
edge = far * green * (ratio - 1.0 / ratio)
log_ratio = math.log(ratio)


def powers(count):
    size = jnp.exp(count.astype(jnp.float32) * log_ratio)
    return jnp.where((count & 1) == 0, size, -size)


def weights(d):
    size = jnp.abs(d)
    value = tail * powers(size) + jnp.where(size == 1, edge, 0.0)
    return jnp.where(d > 0, value, jnp.where(d < 0, -value, 0.0))


def iota(shape, dim):
    return lax.broadcasted_iota(jnp.int32, shape, dim)


def split(x):
    high = x.astype(jnp.bfloat16)
    return high, (x - high.astype(jnp.float32)).astype(jnp.bfloat16)


def dot(a, b, dims=((1,), (0,))):
    return lax.dot_general(a, b, (dims, ((), ())), preferred_element_type=jnp.float32)


def kernel(
    planes, v_hbm, dy_hbm, dz_hbm,
    v, dy, dz, y_out, y_in, z_out, z_in, load_sem, store_sem, send_sem, recv_sem,
):
    rows, nz = v.shape
    ny = rows // planes
    half = y_out.shape[0] // 2
    gy, gz = lax.axis_size("gy"), lax.axis_size("gz")
    iy, iz = lax.axis_index("gy"), lax.axis_index("gz")
    y_next = (lax.rem(iy + 1, gy), iz)
    y_prev = (lax.rem(iy + gy - 1, gy), iz)
    z_next = (iy, lax.rem(iz + 1, gz))
    z_prev = (iy, lax.rem(iz + gz - 1, gz))

    barrier = pltpu.get_barrier_semaphore()
    for other in (y_prev, y_next, z_prev, z_next):
        pl.semaphore_signal(barrier, inc=1, device_id=other, device_id_type=MESH)
    load = pltpu.make_async_copy(v_hbm, v, load_sem)
    load.start()

    place = iota((ny, nz), 0)
    to_next_y = powers(ny - 1 - place)
    to_prev_y = powers(place)
    which, k = iota((16, nz), 0), iota((16, nz), 1)
    message = jnp.where(which == 0, powers(nz - 1 - k), 0.0)
    message = jnp.where((which == 1) & (k == nz - 1), 1.0, message)
    message = jnp.where(which == 8, powers(k), message)
    message = jnp.where((which == 9) & (k == 0), 1.0, message)
    message_hi, message_lo = split(message)
    y_out[...] = jnp.zeros_like(y_out)
    load.wait()

    for p in range(planes):
        plane = v[p * ny:(p + 1) * ny, :]
        y_out[p:p + 1, :] = jnp.sum(plane * to_next_y, axis=0, keepdims=True)
        y_out[planes + p:planes + p + 1, :] = plane[ny - 1:ny, :]
        y_out[half + p:half + p + 1, :] = jnp.sum(plane * to_prev_y, axis=0, keepdims=True)
        y_out[half + planes + p:half + planes + p + 1, :] = plane[0:1, :]
    v_hi, v_lo = split(v[...])
    nt = ((1,), (1,))
    z_out[...] = dot(message_hi, v_hi, nt) + (dot(message_lo, v_hi, nt) + dot(message_hi, v_lo, nt))

    pl.semaphore_wait(barrier, 4)
    copies = []
    for index, (source, target, start, count, other) in enumerate((
        (y_out, y_in, 0, half, y_next),
        (y_out, y_in, half, half, y_prev),
        (z_out, z_in, 0, 8, z_next),
        (z_out, z_in, 8, 8, z_prev),
    )):
        copies.append(pltpu.make_async_remote_copy(
            src_ref=source.at[pl.ds(start, count)],
            dst_ref=target.at[pl.ds(start, count)],
            send_sem=send_sem.at[index],
            recv_sem=recv_sem.at[index],
            device_id=other,
            device_id_type=MESH,
        ))
        copies[-1].start()

    solve_y = weights(iota((ny, ny), 0) - iota((ny, ny), 1))
    y_hi, y_lo = split(solve_y)
    for p in range(planes):
        plane_hi = v_hi[p * ny:(p + 1) * ny, :]
        plane_lo = v_lo[p * ny:(p + 1) * ny, :]
        dy[p * ny:(p + 1) * ny, :] = dot(y_hi, plane_hi) + (dot(y_lo, plane_hi) + dot(y_hi, plane_lo))
    solve_z = weights(iota((nz, nz), 1) - iota((nz, nz), 0))
    z_hi, z_lo = split(solve_z)
    dz[...] = dot(v_hi, z_hi) + (dot(v_lo, z_hi) + dot(v_hi, z_lo))

    spread = jnp.where(which == 0, tail * powers(k + 1), 0.0)
    spread = jnp.where((which == 1) & (k == 0), edge, spread)
    spread = jnp.where(which == 8, -tail * powers(nz - k), spread)
    spread = jnp.where((which == 9) & (k == nz - 1), -edge, spread)
    spread_hi, spread_lo = split(spread)
    from_prev_y = tail * powers(place + 1)
    from_next_y = -tail * powers(ny - place)
    first = jnp.where(iota((8, nz), 0) == 0, edge, 0.0)
    last = jnp.where(iota((8, nz), 0) == 7, -edge, 0.0)

    copies[0].wait_recv()
    copies[1].wait_recv()
    for p in range(planes):
        low, low_edge = y_in[p:p + 1, :], y_in[planes + p:planes + p + 1, :]
        high, high_edge = y_in[half + p:half + p + 1, :], y_in[half + planes + p:half + planes + p + 1, :]
        dy[p * ny:(p + 1) * ny, :] += from_prev_y * low + from_next_y * high
        dy[p * ny:p * ny + 8, :] += first * low_edge
        dy[(p + 1) * ny - 8:(p + 1) * ny, :] += last * high_edge
    store_y = pltpu.make_async_copy(dy, dy_hbm, store_sem.at[0])
    store_y.start()

    copies[2].wait_recv()
    copies[3].wait_recv()
    in_hi, in_lo = split(z_in[...])
    tn = ((0,), (0,))
    dz[...] += dot(in_hi, spread_hi, tn) + (dot(in_lo, spread_hi, tn) + dot(in_hi, spread_lo, tn))
    store_z = pltpu.make_async_copy(dz, dz_hbm, store_sem.at[1])
    store_z.start()
    for copy in copies:
        copy.wait_send()
    store_y.wait()
    store_z.wait()


def per_device(velocity):
    planes = velocity.shape[0] * velocity.shape[1]
    ny, nz = velocity.shape[2:]
    flat = jax.ShapeDtypeStruct((planes * ny, nz), jnp.float32)
    half = (2 * planes + 7) // 8 * 8
    block = pltpu.VMEM(flat.shape, jnp.float32)
    deriv_y, deriv_z = pl.pallas_call(
        functools.partial(kernel, planes),
        out_shape=(flat, flat),
        in_specs=[pl.BlockSpec(memory_space=pl.ANY)],
        out_specs=(pl.BlockSpec(memory_space=pl.ANY),) * 2,
        scratch_shapes=[
            block, block, block,
            pltpu.VMEM((2 * half, nz), jnp.float32),
            pltpu.VMEM((2 * half, nz), jnp.float32),
            pltpu.VMEM((16, planes * ny), jnp.float32),
            pltpu.VMEM((16, planes * ny), jnp.float32),
            pltpu.SemaphoreType.DMA,
            pltpu.SemaphoreType.DMA((2,)),
            pltpu.SemaphoreType.DMA((4,)),
            pltpu.SemaphoreType.DMA((4,)),
        ],
        compiler_params=pltpu.CompilerParams(
            collective_id=0, has_side_effects=True, vmem_limit_bytes=16 * 2**20
        ),
        cost_estimate=pl.CostEstimate(
            flops=6 * planes * ny * nz * (ny + nz), bytes_accessed=12 * planes * ny * nz, transcendentals=0
        ),
    )(velocity.reshape(flat.shape))
    return deriv_y.reshape(velocity.shape), deriv_z.reshape(velocity.shape)


def solution(mesh):
    spec = P(None, None, "gy", "gz")
    return jax.shard_map(
        per_device, mesh=mesh, in_specs=(spec,), out_specs=(spec, spec), check_vma=False
    )
```

time: 28.7 us -> 13.2 us (0.46)
  waiting for transfers between devices: 13.2 us -> 0 us
  Pallas kernels: 0 us -> 9.94 us
  starting transfers between devices: 7.97 us -> 0 us
  matrix products: 3.35 us -> 0 us
  other arithmetic: 1.15 us -> 0 us
  local copies, waits for them, and re-layouts: 2.08 us -> 2.48 us
    ppermute x6 -> x0, waiting for transfers between devices: 13.2 us -> none  [the longest x2 9.9 us: shifted(): lax.ppermute(shard, axis, [(i, (i + by) % count) for i in range(count)])]
    pallas_call x0 -> x1, Pallas kernels: none -> 9.94 us  [per_device(): pl.pallas_call(functools.partial(kernel, planes), out_shape=(flat, flat),...]
    ppermute x6 -> x0, starting transfers between devices: 7.97 us -> none  [the longest x2 7.79 us: padded_2(): lax.ppermute(lax.slice_in_dim(block, 0, width, axis=dim), axis, backward)]
    dot_general x3 -> x0, matrix products: 3.35 us -> none  [the longest x1 2.07 us: z_margin(): return jnp.einsum('ij,cxyj->cxyi', window, rhs_cols, precision=best)]
    unnamed x5 -> x4, local copies, waits for them, and re-layouts: 0.04 us -> 2.48 us
    slice x4 -> x0, local copies, waits for them, and re-layouts: 2.03 us -> none  [the longest x1 1.18 us: padded_2(): lax.slice_in_dim(block, block.shape[dim] - width, None, axis=dim)]
    add x2 -> x0, other arithmetic: 0.85 us -> none  [the longest x1 0.85 us: y_chain(): backward + tail_decay[None, None, :, None] * carry_back[:, :, None, :]]
  transfers between devices with their start and end apart: 6 -> 0, of which waited for: 3 -> 0; matrix products, arithmetic and copies ran while one was open for 12% -> 0% of each run, Pallas kernels for 0% -> 0%
where the time goes in v1:
time: 13.2 us; the launch traced here: 13.1 us
  Pallas kernels  9.94 us (75%)
  local copies, waits for them, and re-layouts  2.48 us (19%)
  between operations  0.65 us (5%)
    pallas_call x1, Pallas kernels, per_device(): pl.pallas_call(functools.partial(kernel, planes), out_shape=(flat, flat),...  9.94 us
    unnamed x4, local copies, waits for them, and re-layouts  2.48 us

profile of v1, /device:TPU:0, one launch (start us, length us, event | category | flops | bytes accessed | tf_op | source)
XLA Modules:
  0.0 13.1 jit_solution(18276731634945143097)
XLA Ops:
  0.6 0.0 copy-start
  0.6 1.0 %copy-done = f32[3,2,64,256]{3,2,1,0:T(8,128)S(1)} copy-done((f32[3,2,64,256]{3,2,1,0:T(8,128)S(1)}, f32[3,2,64,256]{3,2,1,0:T(8,128)}, u32[]{:S(2)}) %copy-start) | copy-done | bytes 393240
  1.6 9.9 %shard_map.30 = (f32[384,256]{1,0:T(8,128)S(1)}, f32[384,256]{1,0:T(8,128)S(1)}) custom-call(f32[384,256]{1,0:T(8,128)S(1)} %bitcast.5), custom_call_target="tpu_custom_call" | custom-call | flops 188743680 | bytes 1179648 | tf_op jit(solution)/shard_map/pallas_call | solution.py:155
  11.6 0.7 %copy.5 = f32[3,2,64,256]{3,2,1,0:T(8,128)} copy(f32[3,2,64,256]{3,2,1,0:T(8,128)S(1)} %bitcast.4) | data formatting | bytes 786432
  12.3 0.7 %copy.6 = f32[3,2,64,256]{3,2,1,0:T(8,128)} copy(f32[3,2,64,256]{3,2,1,0:T(8,128)S(1)} %bitcast.3) | data formatting | bytes 786432
Async XLA Ops:
  0.6 1.0 %copy-start = (f32[3,2,64,256]{3,2,1,0:T(8,128)S(1)}, f32[3,2,64,256]{3,2,1,0:T(8,128)}, u32[]{:S(2)}) copy-start(f32[3,2,64,256]{3,2,1,0:T(8,128)} %param.1) | copy-start | bytes 1179652

commit v2 on v1

--- a/solution.py
+++ b/solution.py
@@ -42,10 +42,7 @@
     return lax.dot_general(a, b, (dims, ((), ())), preferred_element_type=jnp.float32)
 
 
-def kernel(
-    planes, v_hbm, dy_hbm, dz_hbm,
-    v, dy, dz, y_out, y_in, z_out, z_in, load_sem, store_sem, send_sem, recv_sem,
-):
+def kernel(planes, v_hbm, dy, dz, v, y_out, y_in, z_out, z_in, load_sem, send_sem, recv_sem):
     rows, nz = v.shape
     ny = rows // planes
     half = y_out.shape[0] // 2
@@ -59,8 +56,11 @@
     barrier = pltpu.get_barrier_semaphore()
     for other in (y_prev, y_next, z_prev, z_next):
         pl.semaphore_signal(barrier, inc=1, device_id=other, device_id_type=MESH)
-    load = pltpu.make_async_copy(v_hbm, v, load_sem)
-    load.start()
+    loads = []
+    for p in range(planes):
+        part = pl.ds(p * ny, ny)
+        loads.append(pltpu.make_async_copy(v_hbm.at[part], v.at[part], load_sem.at[p]))
+        loads[-1].start()
 
     place = iota((ny, nz), 0)
     to_next_y = powers(ny - 1 - place)
@@ -72,9 +72,20 @@
     message = jnp.where((which == 9) & (k == 0), 1.0, message)
     message_hi, message_lo = split(message)
     y_out[...] = jnp.zeros_like(y_out)
-    load.wait()
+    y_hi, y_lo = split(weights(iota((ny, ny), 0) - iota((ny, ny), 1)))
+    z_hi, z_lo = split(weights(iota((nz, nz), 1) - iota((nz, nz), 0)))
+    spread = jnp.where(which == 0, tail * powers(k + 1), 0.0)
+    spread = jnp.where((which == 1) & (k == 0), edge, spread)
+    spread = jnp.where(which == 8, -tail * powers(nz - k), spread)
+    spread = jnp.where((which == 9) & (k == nz - 1), -edge, spread)
+    spread_hi, spread_lo = split(spread)
+    from_prev_y = tail * powers(place + 1)
+    from_next_y = -tail * powers(ny - place)
+    first = jnp.where(iota((8, nz), 0) == 0, edge, 0.0)
+    last = jnp.where(iota((8, nz), 0) == 7, -edge, 0.0)
 
     for p in range(planes):
+        loads[p].wait()
         plane = v[p * ny:(p + 1) * ny, :]
         y_out[p:p + 1, :] = jnp.sum(plane * to_next_y, axis=0, keepdims=True)
         y_out[planes + p:planes + p + 1, :] = plane[ny - 1:ny, :]
@@ -102,25 +113,17 @@
         ))
         copies[-1].start()
 
-    solve_y = weights(iota((ny, ny), 0) - iota((ny, ny), 1))
-    y_hi, y_lo = split(solve_y)
     for p in range(planes):
         plane_hi = v_hi[p * ny:(p + 1) * ny, :]
         plane_lo = v_lo[p * ny:(p + 1) * ny, :]
         dy[p * ny:(p + 1) * ny, :] = dot(y_hi, plane_hi) + (dot(y_lo, plane_hi) + dot(y_hi, plane_lo))
-    solve_z = weights(iota((nz, nz), 1) - iota((nz, nz), 0))
-    z_hi, z_lo = split(solve_z)
     dz[...] = dot(v_hi, z_hi) + (dot(v_lo, z_hi) + dot(v_hi, z_lo))
 
-    spread = jnp.where(which == 0, tail * powers(k + 1), 0.0)
-    spread = jnp.where((which == 1) & (k == 0), edge, spread)
-    spread = jnp.where(which == 8, -tail * powers(nz - k), spread)
-    spread = jnp.where((which == 9) & (k == nz - 1), -edge, spread)
-    spread_hi, spread_lo = split(spread)
-    from_prev_y = tail * powers(place + 1)
-    from_next_y = -tail * powers(ny - place)
-    first = jnp.where(iota((8, nz), 0) == 0, edge, 0.0)
-    last = jnp.where(iota((8, nz), 0) == 7, -edge, 0.0)
+    copies[2].wait_recv()
+    copies[3].wait_recv()
+    in_hi, in_lo = split(z_in[...])
+    tn = ((0,), (0,))
+    dz[...] += dot(in_hi, spread_hi, tn) + (dot(in_lo, spread_hi, tn) + dot(in_hi, spread_lo, tn))
 
     copies[0].wait_recv()
     copies[1].wait_recv()
@@ -130,51 +133,57 @@
         dy[p * ny:(p + 1) * ny, :] += from_prev_y * low + from_next_y * high
         dy[p * ny:p * ny + 8, :] += first * low_edge
         dy[(p + 1) * ny - 8:(p + 1) * ny, :] += last * high_edge
-    store_y = pltpu.make_async_copy(dy, dy_hbm, store_sem.at[0])
-    store_y.start()
-
-    copies[2].wait_recv()
-    copies[3].wait_recv()
-    in_hi, in_lo = split(z_in[...])
-    tn = ((0,), (0,))
-    dz[...] += dot(in_hi, spread_hi, tn) + (dot(in_lo, spread_hi, tn) + dot(in_hi, spread_lo, tn))
-    store_z = pltpu.make_async_copy(dz, dz_hbm, store_sem.at[1])
-    store_z.start()
     for copy in copies:
         copy.wait_send()
-    store_y.wait()
-    store_z.wait()
+
+
+def store(dy, dz, dy_hbm, dz_hbm, sem):
+    copies = (
+        pltpu.make_async_copy(dy, dy_hbm, sem.at[0]),
+        pltpu.make_async_copy(dz, dz_hbm, sem.at[1]),
+    )
+    for copy in copies:
+        copy.start()
+    for copy in copies:
+        copy.wait()
 
 
 def per_device(velocity):
     planes = velocity.shape[0] * velocity.shape[1]
     ny, nz = velocity.shape[2:]
-    flat = jax.ShapeDtypeStruct((planes * ny, nz), jnp.float32)
+    flat = (planes * ny, nz)
     half = (2 * planes + 7) // 8 * 8
-    block = pltpu.VMEM(flat.shape, jnp.float32)
-    deriv_y, deriv_z = pl.pallas_call(
+    in_vmem = pl.BlockSpec(memory_space=pltpu.VMEM)
+    in_hbm = pl.BlockSpec(memory_space=pltpu.HBM)
+    result = pltpu.VMEM(flat, jnp.float32)
+    parts = pl.pallas_call(
         functools.partial(kernel, planes),
-        out_shape=(flat, flat),
-        in_specs=[pl.BlockSpec(memory_space=pl.ANY)],
-        out_specs=(pl.BlockSpec(memory_space=pl.ANY),) * 2,
+        out_shape=(result, result),
+        in_specs=[in_hbm],
+        out_specs=(in_vmem, in_vmem),
         scratch_shapes=[
-            block, block, block,
+            pltpu.VMEM(flat, jnp.float32),
             pltpu.VMEM((2 * half, nz), jnp.float32),
             pltpu.VMEM((2 * half, nz), jnp.float32),
             pltpu.VMEM((16, planes * ny), jnp.float32),
             pltpu.VMEM((16, planes * ny), jnp.float32),
-            pltpu.SemaphoreType.DMA,
-            pltpu.SemaphoreType.DMA((2,)),
+            pltpu.SemaphoreType.DMA((planes,)),
             pltpu.SemaphoreType.DMA((4,)),
             pltpu.SemaphoreType.DMA((4,)),
         ],
         compiler_params=pltpu.CompilerParams(
             collective_id=0, has_side_effects=True, vmem_limit_bytes=16 * 2**20
         ),
-        cost_estimate=pl.CostEstimate(
-            flops=6 * planes * ny * nz * (ny + nz), bytes_accessed=12 * planes * ny * nz, transcendentals=0
-        ),
-    )(velocity.reshape(flat.shape))
+    )(pltpu.with_memory_space_constraint(velocity.reshape(flat), pltpu.HBM))
+    stored = pltpu.HBM(flat, jnp.float32)
+    deriv_y, deriv_z = pl.pallas_call(
+        store,
+        out_shape=(stored, stored),
+        in_specs=[in_vmem, in_vmem],
+        out_specs=(in_hbm, in_hbm),
+        scratch_shapes=[pltpu.SemaphoreType.DMA((2,))],
+        compiler_params=pltpu.CompilerParams(vmem_limit_bytes=4 * 2**20),
+    )(*(pltpu.with_memory_space_constraint(part, pltpu.VMEM) for part in parts))
     return deriv_y.reshape(velocity.shape), deriv_z.reshape(velocity.shape)
 
 

time: 13.2 us -> 11.2 us (0.85)
  the two profiles are of different devices: /device:TPU:0 before, /device:TPU:1 now
where the time goes in v2:
time: 11.2 us; the launch traced here: 11 us
  Pallas kernels  10.4 us (93%)
  between operations  0.64 us (6%)
    pallas_call x1, Pallas kernels, per_device(): pl.pallas_call(functools.partial(kernel, planes), out_shape=(result, resu...  9.51 us
    pallas_call x1, Pallas kernels, per_device(): pl.pallas_call(store, out_shape=(stored, stored), in_specs=[in_vmem, in_v...  0.89 us

profile of v2, /device:TPU:1, one launch (start us, length us, event | category | flops | bytes accessed | tf_op | source)
XLA Modules:
  0.0 11.0 jit_solution(1920565984078497018)
XLA Ops:
  0.6 9.5 %shard_map.30 = (f32[384,256]{1,0:T(8,128)S(1)}, f32[384,256]{1,0:T(8,128)S(1)}) custom-call(f32[384,256]{1,0:T(8,128)} %bitcast.3), custom_call_target="tpu_custom_call" | custom-call | tf_op jit(solution)/shard_map/pallas_call | solution.py:159
  10.1 0.9 %shard_map.31 = (f32[384,256]{1,0:T(8,128)}, f32[384,256]{1,0:T(8,128)}) custom-call(f32[384,256]{1,0:T(8,128)S(1)} %get-tuple-element.6.dy, f32[384,256]{1,0:T(8,128)S(1)} %get-tuple-element.7.dz), custom_call_target="tpu_custom_call" | custom-call | tf_op jit(solution)/shard_map/pallas_call | solution.py:179

commit v3 on v2

v3 whole, which is shorter than its diff:
```python
import functools
import math

import jax
import jax.numpy as jnp
from jax import lax
from jax.experimental import pallas as pl
from jax.experimental.pallas import tpu as pltpu
from jax.sharding import PartitionSpec as P

MESH = pl.DeviceIdType.MESH
ratio = 1.5 - math.sqrt(5.0) / 2.0
near = 7.0 / 9.0
far = 1.0 / 36.0
green = 1.0 / (1.0 - 2.0 / 3.0 * ratio)
tail = green * (near * (1.0 / ratio - ratio) + far * (ratio**2 - 1.0 / ratio**2))
edge = far * green * (ratio - 1.0 / ratio)
log_ratio = math.log(ratio)


def powers(count):
    size = jnp.exp(count.astype(jnp.float32) * log_ratio)
    return jnp.where((count & 1) == 0, size, -size)


def weights(d):
    size = jnp.abs(d)
    value = tail * powers(size) + jnp.where(size == 1, edge, 0.0)
    return jnp.where(d > 0, value, jnp.where(d < 0, -value, 0.0))


def iota(shape, dim):
    return lax.broadcasted_iota(jnp.int32, shape, dim)


def split(x):
    high = x.astype(jnp.bfloat16)
    return high, (x - high.astype(jnp.float32)).astype(jnp.bfloat16)


def dot(a, b, dims=((1,), (0,))):
    return lax.dot_general(a, b, (dims, ((), ())), preferred_element_type=jnp.float32)


def exchange(planes, v_hbm, dy, dz, y_in, z_in, v, y_out, z_out, load_sem, send_sem, recv_sem):
    rows, nz = v.shape
    ny = rows // planes
    half = y_out.shape[0] // 2
    gy, gz = lax.axis_size("gy"), lax.axis_size("gz")
    iy, iz = lax.axis_index("gy"), lax.axis_index("gz")
    y_next = (lax.rem(iy + 1, gy), iz)
    y_prev = (lax.rem(iy + gy - 1, gy), iz)
    z_next = (iy, lax.rem(iz + 1, gz))
    z_prev = (iy, lax.rem(iz + gz - 1, gz))

    barrier = pltpu.get_barrier_semaphore()
    for other in (y_prev, y_next, z_prev, z_next):
        pl.semaphore_signal(barrier, inc=1, device_id=other, device_id_type=MESH)
    loads = []
    for p in range(planes):
        part = pl.ds(p * ny, ny)
        loads.append(pltpu.make_async_copy(v_hbm.at[part], v.at[part], load_sem.at[p]))
        loads[-1].start()

    def send(index, source, target, start, count, other):
        copy = pltpu.make_async_remote_copy(
            src_ref=source.at[pl.ds(start, count)],
            dst_ref=target.at[pl.ds(start, count)],
            send_sem=send_sem.at[index],
            recv_sem=recv_sem.at[index],
            device_id=other,
            device_id_type=MESH,
        )
        copy.start()
        return copy

    place = iota((ny, nz), 0)
    to_next_y = powers(ny - 1 - place)
    to_prev_y = powers(place)
    which, k = iota((16, nz), 0), iota((16, nz), 1)
    message = jnp.where(which == 0, powers(nz - 1 - k), 0.0)
    message = jnp.where((which == 1) & (k == nz - 1), 1.0, message)
    message = jnp.where(which == 8, powers(k), message)
    message = jnp.where((which == 9) & (k == 0), 1.0, message)
    message_hi, message_lo = split(message)
    message_both = jnp.concatenate([message_hi, message_lo], axis=0)
    y_out[...] = jnp.zeros_like(y_out)
    y_hi, y_lo = split(weights(iota((ny, ny), 0) - iota((ny, ny), 1)))
    z_hi, z_lo = split(weights(iota((nz, nz), 1) - iota((nz, nz), 0)))

    for p in range(planes):
        loads[p].wait()
        plane = v[p * ny:(p + 1) * ny, :]
        y_out[p:p + 1, :] = jnp.sum(plane * to_next_y, axis=0, keepdims=True)
        y_out[planes + p:planes + p + 1, :] = plane[ny - 1:ny, :]
        y_out[half + p:half + p + 1, :] = jnp.sum(plane * to_prev_y, axis=0, keepdims=True)
        y_out[half + planes + p:half + planes + p + 1, :] = plane[0:1, :]
    pl.semaphore_wait(barrier, 4)
    copies = [
        send(0, y_out, y_in, 0, half, y_next),
        send(1, y_out, y_in, half, half, y_prev),
    ]
    v_hi, v_lo = split(v[...])
    nt = ((1,), (1,))
    both = dot(message_both, v_hi, nt)
    z_out[...] = both[:16] + (both[16:] + dot(message_hi, v_lo, nt))
    copies.append(send(2, z_out, z_in, 0, 8, z_next))
    copies.append(send(3, z_out, z_in, 8, 8, z_prev))

    for p in range(planes):
        plane_hi = v_hi[p * ny:(p + 1) * ny, :]
        plane_lo = v_lo[p * ny:(p + 1) * ny, :]
        dy[p * ny:(p + 1) * ny, :] = dot(y_hi, plane_hi) + (dot(y_lo, plane_hi) + dot(y_hi, plane_lo))
    dz[...] = dot(v_hi, z_hi) + (dot(v_lo, z_hi) + dot(v_hi, z_lo))

    for copy in copies:
        copy.wait()


def finish(planes, own_y, own_z, y_in, z_in, dy_hbm, dz_hbm, dy, dz, y_sem, z_sem):
    rows, nz = own_z.shape
    ny = rows // planes
    half = y_in.shape[0] // 2
    which, k = iota((16, nz), 0), iota((16, nz), 1)
    spread = jnp.where(which == 0, tail * powers(k + 1), 0.0)
    spread = jnp.where((which == 1) & (k == 0), edge, spread)
    spread = jnp.where(which == 8, -tail * powers(nz - k), spread)
    spread = jnp.where((which == 9) & (k == nz - 1), -edge, spread)
    spread_hi, spread_lo = split(spread)
    in_hi, in_lo = split(z_in[...])
    z_part = dot(
        jnp.concatenate([in_hi, in_lo, in_hi], axis=0),
        jnp.concatenate([spread_hi, spread_hi, spread_lo], axis=0),
        ((0,), (0,)),
    )
    place = iota((ny, nz), 0)
    from_prev_y = tail * powers(place + 1)
    from_next_y = -tail * powers(ny - place)
    first = jnp.where(place == 0, edge, 0.0)
    last = jnp.where(place == ny - 1, -edge, 0.0)
    copies = []

    def store(source, target, p, sem):
        part = pl.ds(p * ny, ny)
        copies.append(pltpu.make_async_copy(source.at[part], target.at[part], sem.at[p]))
        copies[-1].start()

    for p in range(planes):
        low, low_edge = y_in[p:p + 1, :], y_in[planes + p:planes + p + 1, :]
        high, high_edge = y_in[half + p:half + p + 1, :], y_in[half + planes + p:half + planes + p + 1, :]
        part = slice(p * ny, (p + 1) * ny)
        dy[part, :] = (own_y[part, :] + (from_prev_y * low + from_next_y * high)) + (first * low_edge + last * high_edge)
        store(dy, dy_hbm, p, y_sem)
    for p in range(planes):
        part = slice(p * ny, (p + 1) * ny)
        dz[part, :] = own_z[part, :] + z_part[part, :]
        store(dz, dz_hbm, p, z_sem)
    for copy in copies:
        copy.wait()


def per_device(velocity):
    planes = velocity.shape[0] * velocity.shape[1]
    ny, nz = velocity.shape[2:]
    flat = (planes * ny, nz)
    half = (2 * planes + 7) // 8 * 8
    block = pltpu.VMEM(flat, jnp.float32)
    y_message = pltpu.VMEM((2 * half, nz), jnp.float32)
    z_message = pltpu.VMEM((16, planes * ny), jnp.float32)
    in_vmem = pl.BlockSpec(memory_space=pltpu.VMEM)
    in_hbm = pl.BlockSpec(memory_space=pltpu.HBM)
    parts = pl.pallas_call(
        functools.partial(exchange, planes),
        out_shape=(block, block, y_message, z_message),
        in_specs=[in_hbm],
        out_specs=(in_vmem,) * 4,
        scratch_shapes=[
            block, y_message, z_message,
            pltpu.SemaphoreType.DMA((planes,)),
            pltpu.SemaphoreType.DMA((4,)),
            pltpu.SemaphoreType.DMA((4,)),
        ],
        compiler_params=pltpu.CompilerParams(
            collective_id=0, has_side_effects=True, vmem_limit_bytes=16 * 2**20
        ),
    )(pltpu.with_memory_space_constraint(velocity.reshape(flat), pltpu.HBM))
    stored = pltpu.HBM(flat, jnp.float32)
    deriv_y, deriv_z = pl.pallas_call(
        functools.partial(finish, planes),
        out_shape=(stored, stored),
        in_specs=[in_vmem] * 4,
        out_specs=(in_hbm, in_hbm),
        scratch_shapes=[
            block, block,
            pltpu.SemaphoreType.DMA((planes,)),
            pltpu.SemaphoreType.DMA((planes,)),
        ],
        compiler_params=pltpu.CompilerParams(vmem_limit_bytes=16 * 2**20),
    )(*(pltpu.with_memory_space_constraint(part, pltpu.VMEM) for part in parts))
    return deriv_y.reshape(velocity.shape), deriv_z.reshape(velocity.shape)


def solution(mesh):
    spec = P(None, None, "gy", "gz")
    return jax.shard_map(
        per_device, mesh=mesh, in_specs=(spec,), out_specs=(spec, spec), check_vma=False
    )
```

time: 11.2 us -> 10.9 us (0.973)
  the two profiles are of different devices: /device:TPU:1 before, /device:TPU:0 now
where the time goes in v3:
time: 10.9 us; the launch traced here: 10.8 us
  Pallas kernels  10.1 us (93%)
  between operations  0.64 us (6%)
    pallas_call x1, Pallas kernels, per_device(): pl.pallas_call(functools.partial(exchange, planes), out_shape=(block, blo...  8.97 us
    pallas_call x1, Pallas kernels, per_device(): pl.pallas_call(functools.partial(finish, planes), out_shape=(stored, stor...  1.17 us

profile of v3, /device:TPU:0, one launch (start us, length us, event | category | flops | bytes accessed | tf_op | source)
XLA Modules:
  0.0 10.8 jit_solution(677870084290165655)
XLA Ops:
  0.6 9.0 %shard_map.30 = (f32[384,256]{1,0:T(8,128)S(1)}, f32[384,256]{1,0:T(8,128)S(1)}, f32[32,256]{1,0:T(8,128)S(1)}, f32[16,384]{1,0:T(8,128)S(1)}) custom-call(f32[384,256]{1,0:T(8,128)} %bitcast.3), custom_call_target="tpu_custom_call" | custom-call | tf_op jit(solution)/shard_map/pallas_call | solution.py:172
  9.6 1.2 %shard_map.31 = (f32[384,256]{1,0:T(8,128)}, f32[384,256]{1,0:T(8,128)}) custom-call(f32[384,256]{1,0:T(8,128)S(1)} %get-tuple-element.8.own_y, f32[384,256]{1,0:T(8,128)S(1)} %get-tuple-element.9.own_z, f32[32,256]{1,0:T(8,128)S(1)} %get-tuple-element.10.y_in, f32[16,384]{1,0:T(8,128)S(1)} %get-tuple-element.11.z_in), custom_call_target="tpu_custom_call" | custom-call | tf_op jit(solution)/shard_map/pallas_call | solution.py:188

commit v4 on v3

--- a/solution.py
+++ b/solution.py
@@ -42,7 +42,18 @@
     return lax.dot_general(a, b, (dims, ((), ())), preferred_element_type=jnp.float32)
 
 
-def exchange(planes, v_hbm, dy, dz, y_in, z_in, v, y_out, z_out, load_sem, send_sem, recv_sem):
+def put_row(ref, start, planes, p, row):
+    for c in range(row.shape[1] // 128):
+        place = start + c * planes + p
+        ref[place:place + 1, :] = row[:, c * 128:(c + 1) * 128]
+
+
+def get_row(ref, start, planes, p, nz):
+    places = [start + c * planes + p for c in range(nz // 128)]
+    return jnp.concatenate([ref[place:place + 1, :] for place in places], axis=1)
+
+
+def exchange(planes, v_hbm, dy, dz, y_in, y_weight, v, y_out, z_out, z_in, load_sem, send_sem, recv_sem):
     rows, nz = v.shape
     ny = rows // planes
     half = y_out.shape[0] // 2
@@ -84,17 +95,26 @@
     message = jnp.where((which == 9) & (k == 0), 1.0, message)
     message_hi, message_lo = split(message)
     message_both = jnp.concatenate([message_hi, message_lo], axis=0)
-    y_out[...] = jnp.zeros_like(y_out)
     y_hi, y_lo = split(weights(iota((ny, ny), 0) - iota((ny, ny), 1)))
     z_hi, z_lo = split(weights(iota((nz, nz), 1) - iota((nz, nz), 0)))
 
+    spread = jnp.where(which == 0, tail * powers(k + 1), 0.0)
+    spread = jnp.where((which == 1) & (k == 0), edge, spread)
+    spread = jnp.where(which == 8, -tail * powers(nz - k), spread)
+    spread = jnp.where((which == 9) & (k == nz - 1), -edge, spread)
+    spread_hi, spread_lo = split(spread)
+    if half > 2 * planes * (nz // 128):
+        y_out[...] = jnp.zeros_like(y_out)
+    y_weight[:ny, :] = tail * powers(place + 1)
+    y_weight[ny:, :] = -tail * powers(ny - place)
+
     for p in range(planes):
         loads[p].wait()
         plane = v[p * ny:(p + 1) * ny, :]
-        y_out[p:p + 1, :] = jnp.sum(plane * to_next_y, axis=0, keepdims=True)
-        y_out[planes + p:planes + p + 1, :] = plane[ny - 1:ny, :]
-        y_out[half + p:half + p + 1, :] = jnp.sum(plane * to_prev_y, axis=0, keepdims=True)
-        y_out[half + planes + p:half + planes + p + 1, :] = plane[0:1, :]
+        put_row(y_out, 0, planes, p, jnp.sum(plane * to_next_y, axis=0, keepdims=True))
+        put_row(y_out, nz // 128 * planes, planes, p, plane[ny - 1:ny, :])
+        put_row(y_out, half, planes, p, jnp.sum(plane * to_prev_y, axis=0, keepdims=True))
+        put_row(y_out, half + nz // 128 * planes, planes, p, plane[0:1, :])
     pl.semaphore_wait(barrier, 4)
     copies = [
         send(0, y_out, y_in, 0, half, y_next),
@@ -113,31 +133,24 @@
         dy[p * ny:(p + 1) * ny, :] = dot(y_hi, plane_hi) + (dot(y_lo, plane_hi) + dot(y_hi, plane_lo))
     dz[...] = dot(v_hi, z_hi) + (dot(v_lo, z_hi) + dot(v_hi, z_lo))
 
-    for copy in copies:
-        copy.wait()
-
-
-def finish(planes, own_y, own_z, y_in, z_in, dy_hbm, dz_hbm, dy, dz, y_sem, z_sem):
-    rows, nz = own_z.shape
-    ny = rows // planes
-    half = y_in.shape[0] // 2
-    which, k = iota((16, nz), 0), iota((16, nz), 1)
-    spread = jnp.where(which == 0, tail * powers(k + 1), 0.0)
-    spread = jnp.where((which == 1) & (k == 0), edge, spread)
-    spread = jnp.where(which == 8, -tail * powers(nz - k), spread)
-    spread = jnp.where((which == 9) & (k == nz - 1), -edge, spread)
-    spread_hi, spread_lo = split(spread)
+    copies[2].wait_recv()
+    copies[3].wait_recv()
     in_hi, in_lo = split(z_in[...])
-    z_part = dot(
+    dz[...] += dot(
         jnp.concatenate([in_hi, in_lo, in_hi], axis=0),
         jnp.concatenate([spread_hi, spread_hi, spread_lo], axis=0),
         ((0,), (0,)),
     )
-    place = iota((ny, nz), 0)
-    from_prev_y = tail * powers(place + 1)
-    from_next_y = -tail * powers(ny - place)
-    first = jnp.where(place == 0, edge, 0.0)
-    last = jnp.where(place == ny - 1, -edge, 0.0)
+    copies[0].wait_recv()
+    copies[1].wait_recv()
+    for copy in copies:
+        copy.wait_send()
+
+
+def finish(planes, own_y, dz, y_in, y_weight, dy_hbm, dz_hbm, dy, y_sem, z_sem):
+    rows, nz = own_y.shape
+    ny = rows // planes
+    half = y_in.shape[0] // 2
     copies = []
 
     def store(source, target, p, sem):
@@ -146,15 +159,20 @@
         copies[-1].start()
 
     for p in range(planes):
-        low, low_edge = y_in[p:p + 1, :], y_in[planes + p:planes + p + 1, :]
-        high, high_edge = y_in[half + p:half + p + 1, :], y_in[half + planes + p:half + planes + p + 1, :]
+        store(dz, dz_hbm, p, z_sem)
+    from_prev_y, from_next_y = y_weight[:ny, :], y_weight[ny:, :]
+    first = jnp.where(iota((8, nz), 0) == 0, edge, 0.0)
+    last = jnp.where(iota((8, nz), 0) == 7, -edge, 0.0)
+    for p in range(planes):
+        low = get_row(y_in, 0, planes, p, nz)
+        low_edge = get_row(y_in, nz // 128 * planes, planes, p, nz)
+        high = get_row(y_in, half, planes, p, nz)
+        high_edge = get_row(y_in, half + nz // 128 * planes, planes, p, nz)
         part = slice(p * ny, (p + 1) * ny)
-        dy[part, :] = (own_y[part, :] + (from_prev_y * low + from_next_y * high)) + (first * low_edge + last * high_edge)
+        dy[part, :] = own_y[part, :] + (from_prev_y * low + from_next_y * high)
+        dy[p * ny:p * ny + 8, :] += first * low_edge
+        dy[(p + 1) * ny - 8:(p + 1) * ny, :] += last * high_edge
         store(dy, dy_hbm, p, y_sem)
-    for p in range(planes):
-        part = slice(p * ny, (p + 1) * ny)
-        dz[part, :] = own_z[part, :] + z_part[part, :]
-        store(dz, dz_hbm, p, z_sem)
     for copy in copies:
         copy.wait()
 
@@ -163,19 +181,19 @@
     planes = velocity.shape[0] * velocity.shape[1]
     ny, nz = velocity.shape[2:]
     flat = (planes * ny, nz)
-    half = (2 * planes + 7) // 8 * 8
+    half = (2 * planes * (nz // 128) + 7) // 8 * 8
     block = pltpu.VMEM(flat, jnp.float32)
-    y_message = pltpu.VMEM((2 * half, nz), jnp.float32)
+    y_message = pltpu.VMEM((2 * half, 128), jnp.float32)
     z_message = pltpu.VMEM((16, planes * ny), jnp.float32)
     in_vmem = pl.BlockSpec(memory_space=pltpu.VMEM)
     in_hbm = pl.BlockSpec(memory_space=pltpu.HBM)
     parts = pl.pallas_call(
         functools.partial(exchange, planes),
-        out_shape=(block, block, y_message, z_message),
+        out_shape=(block, block, y_message, pltpu.VMEM((2 * ny, nz), jnp.float32)),
         in_specs=[in_hbm],
         out_specs=(in_vmem,) * 4,
         scratch_shapes=[
-            block, y_message, z_message,
+            block, y_message, z_message, z_message,
             pltpu.SemaphoreType.DMA((planes,)),
             pltpu.SemaphoreType.DMA((4,)),
             pltpu.SemaphoreType.DMA((4,)),
@@ -191,7 +209,7 @@
         in_specs=[in_vmem] * 4,
         out_specs=(in_hbm, in_hbm),
         scratch_shapes=[
-            block, block,
+            block,
             pltpu.SemaphoreType.DMA((planes,)),
             pltpu.SemaphoreType.DMA((planes,)),
         ],

time: 10.9 us -> 11 us (level)
  the two profiles are of different devices: /device:TPU:0 before, /device:TPU:1 now
where the time goes in v4:
time: 11 us; the launch traced here: 10.8 us
  Pallas kernels  10.2 us (93%)
  between operations  0.64 us (6%)
    pallas_call x1, Pallas kernels, per_device(): pl.pallas_call(functools.partial(exchange, planes), out_shape=(block, blo...  9.22 us
    pallas_call x1, Pallas kernels, per_device(): pl.pallas_call(functools.partial(finish, planes), out_shape=(stored, stor...  0.97 us

profile of v4, /device:TPU:1, one launch (start us, length us, event | category | flops | bytes accessed | tf_op | source)
XLA Modules:
  0.0 10.8 jit_solution(2631557756346515886)
XLA Ops:
  0.6 9.2 %shard_map.30 = (f32[384,256]{1,0:T(8,128)S(1)}, f32[384,256]{1,0:T(8,128)S(1)}, f32[48,128]{1,0:T(8,128)S(1)}, f32[128,256]{1,0:T(8,128)S(1)}) custom-call(f32[384,256]{1,0:T(8,128)} %bitcast.3), custom_call_target="tpu_custom_call" | custom-call | tf_op jit(solution)/shard_map/pallas_call | solution.py:190
  9.9 1.0 %shard_map.31 = (f32[384,256]{1,0:T(8,128)}, f32[384,256]{1,0:T(8,128)}) custom-call(f32[384,256]{1,0:T(8,128)S(1)} %get-tuple-element.8.own_y, f32[384,256]{1,0:T(8,128)S(1)} %get-tuple-element.9.dz, f32[48,128]{1,0:T(8,128)S(1)} %get-tuple-element.10.y_in, f32[128,256]{1,0:T(8,128)S(1)} %get-tuple-element.11.y_weight), custom_call_target="tpu_custom_call" | custom-call | tf_op jit(solution)/shard_map/pallas_call | solution.py:206

commit v5 on v4

--- a/solution.py
+++ b/solution.py
@@ -85,9 +85,9 @@
         copy.start()
         return copy
 
-    place = iota((ny, nz), 0)
-    to_next_y = powers(ny - 1 - place)
-    to_prev_y = powers(place)
+    place = iota((ny, 128), 0)
+    to_next_y = jnp.concatenate([powers(ny - 1 - place)] * (nz // 128), axis=1)
+    to_prev_y = jnp.concatenate([powers(place)] * (nz // 128), axis=1)
     which, k = iota((16, nz), 0), iota((16, nz), 1)
     message = jnp.where(which == 0, powers(nz - 1 - k), 0.0)
     message = jnp.where((which == 1) & (k == nz - 1), 1.0, message)
@@ -105,8 +105,8 @@
     spread_hi, spread_lo = split(spread)
     if half > 2 * planes * (nz // 128):
         y_out[...] = jnp.zeros_like(y_out)
-    y_weight[:ny, :] = tail * powers(place + 1)
-    y_weight[ny:, :] = -tail * powers(ny - place)
+    y_weight[:ny, :] = -tail * ratio * to_prev_y
+    y_weight[ny:, :] = tail * ratio * to_next_y
 
     for p in range(planes):
         loads[p].wait()
@@ -115,15 +115,15 @@
         put_row(y_out, nz // 128 * planes, planes, p, plane[ny - 1:ny, :])
         put_row(y_out, half, planes, p, jnp.sum(plane * to_prev_y, axis=0, keepdims=True))
         put_row(y_out, half + nz // 128 * planes, planes, p, plane[0:1, :])
+    v_hi, v_lo = split(v[...])
+    nt = ((1,), (1,))
+    both = dot(message_both, v_hi, nt)
+    z_out[...] = both[:16] + (both[16:] + dot(message_hi, v_lo, nt))
     pl.semaphore_wait(barrier, 4)
     copies = [
         send(0, y_out, y_in, 0, half, y_next),
         send(1, y_out, y_in, half, half, y_prev),
     ]
-    v_hi, v_lo = split(v[...])
-    nt = ((1,), (1,))
-    both = dot(message_both, v_hi, nt)
-    z_out[...] = both[:16] + (both[16:] + dot(message_hi, v_lo, nt))
     copies.append(send(2, z_out, z_in, 0, 8, z_next))
     copies.append(send(3, z_out, z_in, 8, 8, z_prev))
 

time: 11 us -> 11 us (level)
  the two profiles are of different devices: /device:TPU:1 before, /device:TPU:0 now
where the time goes in v5:
time: 11 us; the launch traced here: 10.8 us
  Pallas kernels  10.2 us (93%)
  between operations  0.64 us (6%)
    pallas_call x1, Pallas kernels, per_device(): pl.pallas_call(functools.partial(exchange, planes), out_shape=(block, blo...  9.19 us
    pallas_call x1, Pallas kernels, per_device(): pl.pallas_call(functools.partial(finish, planes), out_shape=(stored, stor...  0.97 us

profile of v5, /device:TPU:0, one launch (start us, length us, event | category | flops | bytes accessed | tf_op | source)
XLA Modules:
  0.0 10.8 jit_solution(10916408971424087606)
XLA Ops:
  0.6 9.2 %shard_map.30 = (f32[384,256]{1,0:T(8,128)S(1)}, f32[384,256]{1,0:T(8,128)S(1)}, f32[48,128]{1,0:T(8,128)S(1)}, f32[128,256]{1,0:T(8,128)S(1)}) custom-call(f32[384,256]{1,0:T(8,128)} %bitcast.3), custom_call_target="tpu_custom_call" | custom-call | tf_op jit(solution)/shard_map/pallas_call | solution.py:190
  9.8 1.0 %shard_map.31 = (f32[384,256]{1,0:T(8,128)}, f32[384,256]{1,0:T(8,128)}) custom-call(f32[384,256]{1,0:T(8,128)S(1)} %get-tuple-element.8.own_y, f32[384,256]{1,0:T(8,128)S(1)} %get-tuple-element.9.dz, f32[48,128]{1,0:T(8,128)S(1)} %get-tuple-element.10.y_in, f32[128,256]{1,0:T(8,128)S(1)} %get-tuple-element.11.y_weight), custom_call_target="tpu_custom_call" | custom-call | tf_op jit(solution)/shard_map/pallas_call | solution.py:206

commit v6 on v5

--- a/solution.py
+++ b/solution.py
@@ -53,7 +53,7 @@
     return jnp.concatenate([ref[place:place + 1, :] for place in places], axis=1)
 
 
-def exchange(planes, v_hbm, dy, dz, y_in, y_weight, v, y_out, z_out, z_in, load_sem, send_sem, recv_sem):
+def exchange(planes, v_hbm, dy, dz, y_in, y_weight, v, y_out, z_out, z_in, load_sem, send_sem, recv_sem, ready_sem):
     rows, nz = v.shape
     ny = rows // planes
     half = y_out.shape[0] // 2
@@ -64,17 +64,27 @@
     z_next = (iy, lax.rem(iz + 1, gz))
     z_prev = (iy, lax.rem(iz + gz - 1, gz))
 
+    odd = lax.rem(iy, 2) == 1
+    even = lax.rem(iy, 2) == 0
     barrier = pltpu.get_barrier_semaphore()
-    for other in (y_prev, y_next, z_prev, z_next):
-        pl.semaphore_signal(barrier, inc=1, device_id=other, device_id_type=MESH)
+
+    def greet(*others):
+        for other in others:
+            pl.semaphore_signal(barrier, inc=1, device_id=other, device_id_type=MESH)
+
+    @pl.when(even)
+    def _():
+        greet(y_prev, y_next)
+
+    greet(z_prev, z_next)
     loads = []
     for p in range(planes):
         part = pl.ds(p * ny, ny)
         loads.append(pltpu.make_async_copy(v_hbm.at[part], v.at[part], load_sem.at[p]))
         loads[-1].start()
 
-    def send(index, source, target, start, count, other):
-        copy = pltpu.make_async_remote_copy(
+    def message_to(index, source, target, start, count, other):
+        return pltpu.make_async_remote_copy(
             src_ref=source.at[pl.ds(start, count)],
             dst_ref=target.at[pl.ds(start, count)],
             send_sem=send_sem.at[index],
@@ -82,8 +92,6 @@
             device_id=other,
             device_id_type=MESH,
         )
-        copy.start()
-        return copy
 
     place = iota((ny, 128), 0)
     to_next_y = jnp.concatenate([powers(ny - 1 - place)] * (nz // 128), axis=1)
@@ -119,13 +127,27 @@
     nt = ((1,), (1,))
     both = dot(message_both, v_hi, nt)
     z_out[...] = both[:16] + (both[16:] + dot(message_hi, v_lo, nt))
-    pl.semaphore_wait(barrier, 4)
     copies = [
-        send(0, y_out, y_in, 0, half, y_next),
-        send(1, y_out, y_in, half, half, y_prev),
+        message_to(0, y_out, y_in, 0, half, y_next),
+        message_to(1, y_out, y_in, half, half, y_prev),
+        message_to(2, z_out, z_in, 0, 8, z_next),
+        message_to(3, z_out, z_in, 8, 8, z_prev),
     ]
-    copies.append(send(2, z_out, z_in, 0, 8, z_next))
-    copies.append(send(3, z_out, z_in, 8, 8, z_prev))
+
+    @pl.when(odd)
+    def _():
+        pl.semaphore_wait(barrier, 4)
+        pl.semaphore_signal(ready_sem.at[0], inc=1, device_id=y_prev, device_id_type=MESH)
+        pl.semaphore_signal(ready_sem.at[1], inc=1, device_id=y_next, device_id_type=MESH)
+        copies[0].start()
+        copies[1].start()
+
+    @pl.when(even)
+    def _():
+        pl.semaphore_wait(barrier, 2)
+
+    copies[2].start()
+    copies[3].start()
 
     for p in range(planes):
         plane_hi = v_hi[p * ny:(p + 1) * ny, :]
@@ -141,6 +163,14 @@
         jnp.concatenate([spread_hi, spread_hi, spread_lo], axis=0),
         ((0,), (0,)),
     )
+
+    @pl.when(even)
+    def _():
+        pl.semaphore_wait(ready_sem.at[0], 1)
+        copies[0].start()
+        pl.semaphore_wait(ready_sem.at[1], 1)
+        copies[1].start()
+
     copies[0].wait_recv()
     copies[1].wait_recv()
     for copy in copies:
@@ -197,6 +227,7 @@
             pltpu.SemaphoreType.DMA((planes,)),
             pltpu.SemaphoreType.DMA((4,)),
             pltpu.SemaphoreType.DMA((4,)),
+            pltpu.SemaphoreType.REGULAR((2,)),
         ],
         compiler_params=pltpu.CompilerParams(
             collective_id=0, has_side_effects=True, vmem_limit_bytes=16 * 2**20

time: 11 us -> 10.9 us (level)
  no operation moved by 1% of the time
where the time goes in v6:
time: 10.9 us; the launch traced here: 10.7 us
  Pallas kernels  10.1 us (93%)
  between operations  0.64 us (6%)
    pallas_call x1, Pallas kernels, per_device(): pl.pallas_call(functools.partial(exchange, planes), out_shape=(block, blo...  9.11 us
    pallas_call x1, Pallas kernels, per_device(): pl.pallas_call(functools.partial(finish, planes), out_shape=(stored, stor...  0.97 us

profile of v6, /device:TPU:0, one launch (start us, length us, event | category | flops | bytes accessed | tf_op | source)
XLA Modules:
  0.0 10.7 jit_solution(5218619820081346525)
XLA Ops:
  0.6 9.1 %shard_map.30 = (f32[384,256]{1,0:T(8,128)S(1)}, f32[384,256]{1,0:T(8,128)S(1)}, f32[48,128]{1,0:T(8,128)S(1)}, f32[128,256]{1,0:T(8,128)S(1)}) custom-call(f32[384,256]{1,0:T(8,128)} %bitcast.3), custom_call_target="tpu_custom_call" | custom-call | tf_op jit(solution)/shard_map/pallas_call | solution.py:220
  9.7 1.0 %shard_map.31 = (f32[384,256]{1,0:T(8,128)}, f32[384,256]{1,0:T(8,128)}) custom-call(f32[384,256]{1,0:T(8,128)S(1)} %get-tuple-element.8.own_y, f32[384,256]{1,0:T(8,128)S(1)} %get-tuple-element.9.dz, f32[48,128]{1,0:T(8,128)S(1)} %get-tuple-element.10.y_in, f32[128,256]{1,0:T(8,128)S(1)} %get-tuple-element.11.y_weight), custom_call_target="tpu_custom_call" | custom-call | tf_op jit(solution)/shard_map/pallas_call | solution.py:237

commit v7 on v6

--- a/solution.py
+++ b/solution.py
@@ -64,19 +64,25 @@
     z_next = (iy, lax.rem(iz + 1, gz))
     z_prev = (iy, lax.rem(iz + gz - 1, gz))
 
-    odd = lax.rem(iy, 2) == 1
-    even = lax.rem(iy, 2) == 0
+    odd_row = lax.rem(iy, 2) == 1
+    even_row = lax.rem(iy, 2) == 0
+    quick = odd_row & (lax.rem(iz, 2) == 0)
+    full = odd_row & (lax.rem(iz, 2) == 1)
     barrier = pltpu.get_barrier_semaphore()
 
-    def greet(*others):
-        for other in others:
-            pl.semaphore_signal(barrier, inc=1, device_id=other, device_id_type=MESH)
-
-    @pl.when(even)
-    def _():
-        greet(y_prev, y_next)
-
-    greet(z_prev, z_next)
+    def signal(sem, other):
+        pl.semaphore_signal(sem, inc=1, device_id=other, device_id_type=MESH)
+
+    @pl.when(even_row)
+    def _():
+        signal(barrier, y_prev)
+        signal(barrier, y_next)
+
+    @pl.when(even_row | quick)
+    def _():
+        signal(barrier, z_prev)
+        signal(barrier, z_next)
+
     loads = []
     for p in range(planes):
         part = pl.ds(p * ny, ny)
@@ -134,26 +140,43 @@
         message_to(3, z_out, z_in, 8, 8, z_prev),
     ]
 
-    @pl.when(odd)
+    @pl.when(full)
     def _():
         pl.semaphore_wait(barrier, 4)
-        pl.semaphore_signal(ready_sem.at[0], inc=1, device_id=y_prev, device_id_type=MESH)
-        pl.semaphore_signal(ready_sem.at[1], inc=1, device_id=y_next, device_id_type=MESH)
+
+    @pl.when(even_row | quick)
+    def _():
+        pl.semaphore_wait(barrier, 2)
+
+    @pl.when(odd_row)
+    def _():
+        signal(ready_sem.at[0], y_prev)
+        signal(ready_sem.at[1], y_next)
         copies[0].start()
         copies[1].start()
 
-    @pl.when(even)
-    def _():
-        pl.semaphore_wait(barrier, 2)
-
-    copies[2].start()
-    copies[3].start()
+    @pl.when(full)
+    def _():
+        signal(ready_sem.at[2], z_prev)
+        signal(ready_sem.at[3], z_next)
+
+    @pl.when(even_row | full)
+    def _():
+        copies[2].start()
+        copies[3].start()
 
     for p in range(planes):
         plane_hi = v_hi[p * ny:(p + 1) * ny, :]
         plane_lo = v_lo[p * ny:(p + 1) * ny, :]
         dy[p * ny:(p + 1) * ny, :] = dot(y_hi, plane_hi) + (dot(y_lo, plane_hi) + dot(y_hi, plane_lo))
     dz[...] = dot(v_hi, z_hi) + (dot(v_lo, z_hi) + dot(v_hi, z_lo))
+
+    @pl.when(quick)
+    def _():
+        pl.semaphore_wait(ready_sem.at[2], 1)
+        copies[2].start()
+        pl.semaphore_wait(ready_sem.at[3], 1)
+        copies[3].start()
 
     copies[2].wait_recv()
     copies[3].wait_recv()
@@ -164,7 +187,7 @@
         ((0,), (0,)),
     )
 
-    @pl.when(even)
+    @pl.when(even_row)
     def _():
         pl.semaphore_wait(ready_sem.at[0], 1)
         copies[0].start()
@@ -227,7 +250,7 @@
             pltpu.SemaphoreType.DMA((planes,)),
             pltpu.SemaphoreType.DMA((4,)),
             pltpu.SemaphoreType.DMA((4,)),
-            pltpu.SemaphoreType.REGULAR((2,)),
+            pltpu.SemaphoreType.REGULAR((4,)),
         ],
         compiler_params=pltpu.CompilerParams(
             collective_id=0, has_side_effects=True, vmem_limit_bytes=16 * 2**20

time: 10.9 us -> 10.9 us (level)
  no operation moved by 1% of the time
where the time goes in v7:
time: 10.9 us; the launch traced here: 10.7 us
  Pallas kernels  10.1 us (93%)
  between operations  0.64 us (6%)
    pallas_call x1, Pallas kernels, per_device(): pl.pallas_call(functools.partial(exchange, planes), out_shape=(block, blo...  9.13 us
    pallas_call x1, Pallas kernels, per_device(): pl.pallas_call(functools.partial(finish, planes), out_shape=(stored, stor...  0.97 us

profile of v7, /device:TPU:0, one launch (start us, length us, event | category | flops | bytes accessed | tf_op | source)
XLA Modules:
  0.0 10.7 jit_solution(15431449541478894255)
XLA Ops:
  0.6 9.1 %shard_map.30 = (f32[384,256]{1,0:T(8,128)S(1)}, f32[384,256]{1,0:T(8,128)S(1)}, f32[48,128]{1,0:T(8,128)S(1)}, f32[128,256]{1,0:T(8,128)S(1)}) custom-call(f32[384,256]{1,0:T(8,128)} %bitcast.3), custom_call_target="tpu_custom_call" | custom-call | tf_op jit(solution)/shard_map/pallas_call | solution.py:243
  9.8 1.0 %shard_map.31 = (f32[384,256]{1,0:T(8,128)}, f32[384,256]{1,0:T(8,128)}) custom-call(f32[384,256]{1,0:T(8,128)S(1)} %get-tuple-element.8.own_y, f32[384,256]{1,0:T(8,128)S(1)} %get-tuple-element.9.dz, f32[48,128]{1,0:T(8,128)S(1)} %get-tuple-element.10.y_in, f32[128,256]{1,0:T(8,128)S(1)} %get-tuple-element.11.y_weight), custom_call_target="tpu_custom_call" | custom-call | tf_op jit(solution)/shard_map/pallas_call | solution.py:260

commit v8 on v7

--- a/solution.py
+++ b/solution.py
@@ -109,19 +109,8 @@
     message = jnp.where((which == 9) & (k == 0), 1.0, message)
     message_hi, message_lo = split(message)
     message_both = jnp.concatenate([message_hi, message_lo], axis=0)
-    y_hi, y_lo = split(weights(iota((ny, ny), 0) - iota((ny, ny), 1)))
-    z_hi, z_lo = split(weights(iota((nz, nz), 1) - iota((nz, nz), 0)))
-
-    spread = jnp.where(which == 0, tail * powers(k + 1), 0.0)
-    spread = jnp.where((which == 1) & (k == 0), edge, spread)
-    spread = jnp.where(which == 8, -tail * powers(nz - k), spread)
-    spread = jnp.where((which == 9) & (k == nz - 1), -edge, spread)
-    spread_hi, spread_lo = split(spread)
     if half > 2 * planes * (nz // 128):
         y_out[...] = jnp.zeros_like(y_out)
-    y_weight[:ny, :] = -tail * ratio * to_prev_y
-    y_weight[ny:, :] = tail * ratio * to_next_y
-
     for p in range(planes):
         loads[p].wait()
         plane = v[p * ny:(p + 1) * ny, :]
@@ -129,10 +118,6 @@
         put_row(y_out, nz // 128 * planes, planes, p, plane[ny - 1:ny, :])
         put_row(y_out, half, planes, p, jnp.sum(plane * to_prev_y, axis=0, keepdims=True))
         put_row(y_out, half + nz // 128 * planes, planes, p, plane[0:1, :])
-    v_hi, v_lo = split(v[...])
-    nt = ((1,), (1,))
-    both = dot(message_both, v_hi, nt)
-    z_out[...] = both[:16] + (both[16:] + dot(message_hi, v_lo, nt))
     copies = [
         message_to(0, y_out, y_in, 0, half, y_next),
         message_to(1, y_out, y_in, half, half, y_prev),
@@ -140,23 +125,30 @@
         message_to(3, z_out, z_in, 8, 8, z_prev),
     ]
 
-    @pl.when(full)
-    def _():
-        pl.semaphore_wait(barrier, 4)
-
-    @pl.when(even_row | quick)
-    def _():
-        pl.semaphore_wait(barrier, 2)
-
-    @pl.when(odd_row)
-    def _():
+    def send_y():
         signal(ready_sem.at[0], y_prev)
         signal(ready_sem.at[1], y_next)
         copies[0].start()
         copies[1].start()
 
+    @pl.when(quick)
+    def _():
+        pl.semaphore_wait(barrier, 2)
+        send_y()
+
+    v_hi, v_lo = split(v[...])
+    nt = ((1,), (1,))
+    both = dot(message_both, v_hi, nt)
+    z_out[...] = both[:16] + (both[16:] + dot(message_hi, v_lo, nt))
+
+    @pl.when(even_row)
+    def _():
+        pl.semaphore_wait(barrier, 2)
+
     @pl.when(full)
     def _():
+        pl.semaphore_wait(barrier, 4)
+        send_y()
         signal(ready_sem.at[2], z_prev)
         signal(ready_sem.at[3], z_next)
 
@@ -164,6 +156,17 @@
     def _():
         copies[2].start()
         copies[3].start()
+
+    y_hi, y_lo = split(weights(iota((ny, ny), 0) - iota((ny, ny), 1)))
+    z_hi, z_lo = split(weights(iota((nz, nz), 1) - iota((nz, nz), 0)))
+
+    spread = jnp.where(which == 0, tail * powers(k + 1), 0.0)
+    spread = jnp.where((which == 1) & (k == 0), edge, spread)
+    spread = jnp.where(which == 8, -tail * powers(nz - k), spread)
+    spread = jnp.where((which == 9) & (k == nz - 1), -edge, spread)
+    spread_hi, spread_lo = split(spread)
+    y_weight[:ny, :] = -tail * ratio * to_prev_y
+    y_weight[ny:, :] = tail * ratio * to_next_y
 
     for p in range(planes):
         plane_hi = v_hi[p * ny:(p + 1) * ny, :]

time: 10.9 us -> 10.7 us (0.982)
  Pallas kernels: 10.1 us -> 9.89 us
    pallas_call x1, Pallas kernels: 9.13 us -> 8.92 us  [per_device(): pl.pallas_call(functools.partial(exchange, planes), out_shape=(block, blo...]
where the time goes in v8:
time: 10.7 us; the launch traced here: 10.5 us
  Pallas kernels  9.89 us (92%)
  between operations  0.64 us (6%)
    pallas_call x1, Pallas kernels, per_device(): pl.pallas_call(functools.partial(exchange, planes), out_shape=(block, blo...  8.92 us
    pallas_call x1, Pallas kernels, per_device(): pl.pallas_call(functools.partial(finish, planes), out_shape=(stored, stor...  0.97 us

profile of v8, /device:TPU:0, one launch (start us, length us, event | category | flops | bytes accessed | tf_op | source)
XLA Modules:
  0.0 10.5 jit_solution(13902053593148864948)
XLA Ops:
  0.6 8.9 %shard_map.30 = (f32[384,256]{1,0:T(8,128)S(1)}, f32[384,256]{1,0:T(8,128)S(1)}, f32[48,128]{1,0:T(8,128)S(1)}, f32[128,256]{1,0:T(8,128)S(1)}) custom-call(f32[384,256]{1,0:T(8,128)} %bitcast.3), custom_call_target="tpu_custom_call" | custom-call | tf_op jit(solution)/shard_map/pallas_call | solution.py:246
  9.6 1.0 %shard_map.31 = (f32[384,256]{1,0:T(8,128)}, f32[384,256]{1,0:T(8,128)}) custom-call(f32[384,256]{1,0:T(8,128)S(1)} %get-tuple-element.8.own_y, f32[384,256]{1,0:T(8,128)S(1)} %get-tuple-element.9.dz, f32[48,128]{1,0:T(8,128)S(1)} %get-tuple-element.10.y_in, f32[128,256]{1,0:T(8,128)S(1)} %get-tuple-element.11.y_weight), custom_call_target="tpu_custom_call" | custom-call | tf_op jit(solution)/shard_map/pallas_call | solution.py:263

commit v9 on v8

--- a/solution.py
+++ b/solution.py
@@ -126,9 +126,9 @@
     ]
 
     def send_y():
-        signal(ready_sem.at[0], y_prev)
         signal(ready_sem.at[1], y_next)
         copies[0].start()
+        signal(ready_sem.at[0], y_prev)
         copies[1].start()
 
     @pl.when(quick)
@@ -214,8 +214,8 @@
         copies.append(pltpu.make_async_copy(source.at[part], target.at[part], sem.at[p]))
         copies[-1].start()
 
-    for p in range(planes):
-        store(dz, dz_hbm, p, z_sem)
+    copies.append(pltpu.make_async_copy(dz, dz_hbm, z_sem))
+    copies[0].start()
     from_prev_y, from_next_y = y_weight[:ny, :], y_weight[ny:, :]
     first = jnp.where(iota((8, nz), 0) == 0, edge, 0.0)
     last = jnp.where(iota((8, nz), 0) == 7, -edge, 0.0)
@@ -268,7 +268,7 @@
         scratch_shapes=[
             block,
             pltpu.SemaphoreType.DMA((planes,)),
-            pltpu.SemaphoreType.DMA((planes,)),
+            pltpu.SemaphoreType.DMA,
         ],
         compiler_params=pltpu.CompilerParams(vmem_limit_bytes=16 * 2**20),
     )(*(pltpu.with_memory_space_constraint(part, pltpu.VMEM) for part in parts))

time: 10.7 us -> 10.7 us (level)
  no operation moved by 1% of the time
where the time goes in v9:
time: 10.7 us; the launch traced here: 10.5 us
  Pallas kernels  9.85 us (92%)
  between operations  0.64 us (6%)
    pallas_call x1, Pallas kernels, per_device(): pl.pallas_call(functools.partial(exchange, planes), out_shape=(block, blo...  8.92 us
    pallas_call x1, Pallas kernels, per_device(): pl.pallas_call(functools.partial(finish, planes), out_shape=(stored, stor...  0.93 us

profile of v9, /device:TPU:0, one launch (start us, length us, event | category | flops | bytes accessed | tf_op | source)
XLA Modules:
  0.0 10.5 jit_solution(12631603453312269339)
XLA Ops:
  0.6 8.9 %shard_map.30 = (f32[384,256]{1,0:T(8,128)S(1)}, f32[384,256]{1,0:T(8,128)S(1)}, f32[48,128]{1,0:T(8,128)S(1)}, f32[128,256]{1,0:T(8,128)S(1)}) custom-call(f32[384,256]{1,0:T(8,128)} %bitcast.3), custom_call_target="tpu_custom_call" | custom-call | tf_op jit(solution)/shard_map/pallas_call | solution.py:246
  9.6 0.9 %shard_map.31 = (f32[384,256]{1,0:T(8,128)}, f32[384,256]{1,0:T(8,128)}) custom-call(f32[384,256]{1,0:T(8,128)S(1)} %get-tuple-element.8.own_y, f32[384,256]{1,0:T(8,128)S(1)} %get-tuple-element.9.dz, f32[48,128]{1,0:T(8,128)S(1)} %get-tuple-element.10.y_in, f32[128,256]{1,0:T(8,128)S(1)} %get-tuple-element.11.y_weight), custom_call_target="tpu_custom_call" | custom-call | tf_op jit(solution)/shard_map/pallas_call | solution.py:263

commit v10 on v9

--- a/solution.py
+++ b/solution.py
@@ -116,8 +116,6 @@
         plane = v[p * ny:(p + 1) * ny, :]
         put_row(y_out, 0, planes, p, jnp.sum(plane * to_next_y, axis=0, keepdims=True))
         put_row(y_out, nz // 128 * planes, planes, p, plane[ny - 1:ny, :])
-        put_row(y_out, half, planes, p, jnp.sum(plane * to_prev_y, axis=0, keepdims=True))
-        put_row(y_out, half + nz // 128 * planes, planes, p, plane[0:1, :])
     copies = [
         message_to(0, y_out, y_in, 0, half, y_next),
         message_to(1, y_out, y_in, half, half, y_prev),
@@ -125,16 +123,27 @@
         message_to(3, z_out, z_in, 8, 8, z_prev),
     ]
 
-    def send_y():
+    def send_y_next():
         signal(ready_sem.at[1], y_next)
         copies[0].start()
+
+    def send_y_prev():
         signal(ready_sem.at[0], y_prev)
         copies[1].start()
 
     @pl.when(quick)
     def _():
         pl.semaphore_wait(barrier, 2)
-        send_y()
+        send_y_next()
+
+    for p in range(planes):
+        plane = v[p * ny:(p + 1) * ny, :]
+        put_row(y_out, half, planes, p, jnp.sum(plane * to_prev_y, axis=0, keepdims=True))
+        put_row(y_out, half + nz // 128 * planes, planes, p, plane[0:1, :])
+
+    @pl.when(quick)
+    def _():
+        send_y_prev()
 
     v_hi, v_lo = split(v[...])
     nt = ((1,), (1,))
@@ -148,7 +157,8 @@
     @pl.when(full)
     def _():
         pl.semaphore_wait(barrier, 4)
-        send_y()
+        send_y_next()
+        send_y_prev()
         signal(ready_sem.at[2], z_prev)
         signal(ready_sem.at[3], z_next)
 

time: 10.7 us -> 10.7 us (level)
  no operation moved by 1% of the time
where the time goes in v10:
time: 10.7 us; the launch traced here: 10.5 us
  Pallas kernels  9.85 us (92%)
  between operations  0.64 us (6%)
    pallas_call x1, Pallas kernels, per_device(): pl.pallas_call(functools.partial(exchange, planes), out_shape=(block, blo...  8.92 us
    pallas_call x1, Pallas kernels, per_device(): pl.pallas_call(functools.partial(finish, planes), out_shape=(stored, stor...  0.93 us

profile of v10, /device:TPU:0, one launch (start us, length us, event | category | flops | bytes accessed | tf_op | source)
XLA Modules:
  0.0 10.5 jit_solution(5307702193506059218)
XLA Ops:
  0.6 8.9 %shard_map.30 = (f32[384,256]{1,0:T(8,128)S(1)}, f32[384,256]{1,0:T(8,128)S(1)}, f32[48,128]{1,0:T(8,128)S(1)}, f32[128,256]{1,0:T(8,128)S(1)}) custom-call(f32[384,256]{1,0:T(8,128)} %bitcast.3), custom_call_target="tpu_custom_call" | custom-call | tf_op jit(solution)/shard_map/pallas_call | solution.py:256
  9.6 0.9 %shard_map.31 = (f32[384,256]{1,0:T(8,128)}, f32[384,256]{1,0:T(8,128)}) custom-call(f32[384,256]{1,0:T(8,128)S(1)} %get-tuple-element.8.own_y, f32[384,256]{1,0:T(8,128)S(1)} %get-tuple-element.9.dz, f32[48,128]{1,0:T(8,128)S(1)} %get-tuple-element.10.y_in, f32[128,256]{1,0:T(8,128)S(1)} %get-tuple-element.11.y_weight), custom_call_target="tpu_custom_call" | custom-call | tf_op jit(solution)/shard_map/pallas_call | solution.py:273
